TPU v7x, 32 devices: a whole 2x2x4 slice. The times are simulated.
32 devices in a mesh: group: 2 (over x), dx: 16 (over z, y, core).
Axes of the slice: x: 2, y: 2, z: 4, core: 2. Of those that a mesh axis runs over, the one named last changes fastest.
Arguments:
- points: bfloat16 [16384, 1024], P(('group', 'dx')), parts along dimension 0, may hold values from -6 to 6
- cotangent: bfloat16 [16384, 1024], P(('group', 'dx')), parts along dimension 0, may hold values from -96 to 96
- counts: int32 [32], P(('group', 'dx')), parts along dimension 0, may hold values from 170 to 512, as said below
- w_query: bfloat16 [1024, 1024], replicated, may hold values from -0.1875 to 0.1875
- w_key: bfloat16 [1024, 1024], replicated, may hold values from -0.1875 to 0.1875
- w_value: bfloat16 [1024, 1024], replicated, may hold values from -0.1875 to 0.1875
- gain_key: float32 [1024], replicated, may hold values from 0.25 to 1.75
- bias_key: float32 [1024], replicated, may hold values from -3 to 3
- gain_value: float32 [1024], replicated, may hold values from 0.25 to 1.75
- bias_value: float32 [1024], replicated, may hold values from -3 to 3
Outputs:
- grad_points: bfloat16 [16384, 1024], P(('group', 'dx')), parts along dimension 0
There are 2 independent parts, one for each index of `group`. A program takes and returns all parts, laid end to end along the dimension named above; an argument that names none is the same for every part. Nothing has to cross between parts.
Inputs may be any that keep to these rules, and one draw needn't show every extreme that they name: `counts`: live points of each tile; some tile of every slab holds 512.
All inputs are finite; a program needn't handle non-finite values.
Results may differ from a plain program's by a relative error of at most 0.006.
Values sent between devices are 32-bit elements; how exact they have to be, the bound alone decides.
A program may use at most 64 MiB of HBM per device.

v0:
```python
import jax
import jax.numpy as jnp
from jax import lax
from jax.sharding import PartitionSpec as P

HEADS = 8
eps = 1e-05


def head_norm(raw, heads):
    grouped = raw.reshape(raw.shape[0], heads, -1)
    center = grouped - jnp.mean(grouped, axis=2, keepdims=True)
    inverse = lax.rsqrt(jnp.mean(center * center, axis=2, keepdims=True) + eps)
    return (center * inverse, inverse)


def norm_back(grad, gain, normed, inverse, heads):
    scaled = grad * gain.reshape(heads, -1)
    inner = scaled - jnp.mean(scaled, axis=2, keepdims=True)
    inner = inner - normed * jnp.mean(scaled * normed, axis=2, keepdims=True)
    return (inverse * inner).reshape(grad.shape[0], -1).astype(jnp.bfloat16)


def body(
    points, cotangent, counts, w_query, w_key, w_value, gain_key, bias_key, gain_value, bias_value
):
    rows = points.shape[0]
    heads = HEADS
    live = (lax.iota(jnp.int32, rows) < counts[0]).astype(jnp.float32)[:, None]
    live_h = live[:, :, None]
    own_count = counts[0].astype(jnp.float32)
    total = lax.psum(own_count, "dx")
    key_hat, key_inv = head_norm(jnp.dot(points, w_key, preferred_element_type=jnp.float32), heads)
    value_hat, value_inv = head_norm(
        jnp.dot(points, w_value, preferred_element_type=jnp.float32), heads
    )
    keys = (live_h * (key_hat * gain_key.reshape(heads, -1) + bias_key.reshape(heads, -1))).astype(
        jnp.bfloat16
    )
    values = (
        live_h * (value_hat * gain_value.reshape(heads, -1) + bias_value.reshape(heads, -1))
    ).astype(jnp.bfloat16)
    kv_local = jnp.einsum("nhi,nhj->hij", keys, values, preferred_element_type=jnp.float32)
    cot = cotangent.reshape(rows, heads, -1)
    kv_sum = lax.psum(kv_local, "dx")
    query = jnp.dot(points, w_query, preferred_element_type=jnp.float32).astype(jnp.bfloat16)
    masked_query = (query * live.astype(jnp.bfloat16)).reshape(rows, heads, -1)
    qdy_local = jnp.einsum("nhi,nhj->hij", masked_query, cot, preferred_element_type=jnp.float32)
    qdy_sum = lax.psum(qdy_local, "dx")
    gram = (kv_sum / total).astype(jnp.bfloat16)
    dgram = (qdy_sum / total).astype(jnp.bfloat16)
    dquery = (
        (live_h * jnp.einsum("nhj,hij->nhi", cot, gram, preferred_element_type=jnp.float32))
        .reshape(rows, -1)
        .astype(jnp.bfloat16)
    )
    dkeys = jnp.einsum("nhj,hij->nhi", values, dgram, preferred_element_type=jnp.float32)
    dvalues = jnp.einsum("nhi,hij->nhj", keys, dgram, preferred_element_type=jnp.float32)
    dkey_raw = norm_back(dkeys, gain_key, key_hat, key_inv, heads)
    dvalue_raw = norm_back(dvalues, gain_value, value_hat, value_inv, heads)
    grad = jnp.dot(dquery, w_query.T, preferred_element_type=jnp.float32)
    grad = grad + jnp.dot(dkey_raw, w_key.T, preferred_element_type=jnp.float32)
    grad = grad + jnp.dot(dvalue_raw, w_value.T, preferred_element_type=jnp.float32)
    return grad.astype(jnp.bfloat16)


def solution(mesh):
    placed = (
        P(("group", "dx"), None),
        P(("group", "dx"), None),
        P(("group", "dx")),
        P(),
        P(),
        P(),
        P(),
        P(),
        P(),
        P(),
    )
    return jax.shard_map(
        body, mesh=mesh, in_specs=placed, out_specs=P(("group", "dx"), None), check_vma=False
    )
```

profile of v0, /device:TPU:0, one launch (start us, length us, event | category | flops | bytes accessed | tf_op | source)
XLA Modules:
  0.0 156.2 jit_solution(9435731812244880489)
XLA Ops:
  6.5 0.0 copy-start
  6.5 0.0 all-reduce.3.cloned.1.call-start
  6.5 3.3 %convolution_bitcast_fusion = f32[64,8,8,128]{3,1,2,0:T(8,128)S(1)} fusion(bf16[512,1024]{1,0:T(8,128)(2,1)} %param.10, bf16[1024,1024]{1,0:T(8,128)(2,1)} %param.15), kind=kOutput, calls=%fused_computation.22 | convolution fusion | flops 1073741824 | bytes 5242880 | tf_op jit(solution)/shard_map/dot_general | solution.py:35
  9.8 1.8 %copy.72 = f32[64,8,8,128]{3,2,1,0:T(8,128)} copy(f32[64,8,8,128]{3,1,2,0:T(8,128)S(1)} %convolution_bitcast_fusion) | data formatting | bytes 4194304
  11.6 3.0 %copy.57 = f32[512,8,128]{0,2,1:T(8,128)} copy(f32[512,8,128]{2,1,0:T(8,128)} %bitcast.70) | data formatting | bytes 4194304 | tf_op jit(solution)/shard_map/reshape | solution.py:11
  14.6 2.3 %reduce_sum.74 = f32[512,8]{1,0:T(8,128)S(1)} reduce(f32[512,8,128]{2,1,0:T(8,128)} %bitcast.71, f32[]{:T(128)} %constant.11.clone.1), dimensions={2}, to_apply=%region_2.0 | reduce | flops 520192 | bytes 2113540 | tf_op jit(solution)/shard_map/reduce_sum | solution.py:12
  16.9 0.0 copy-done
  16.9 0.0 copy-done.11
  16.9 1.3 convolution_bitcast_fusion.1
  18.2 1.8 %copy.71 = f32[64,8,8,128]{3,2,1,0:T(8,128)} copy(f32[64,8,8,128]{3,1,2,0:T(8,128)S(1)} %convolution_bitcast_fusion.1) | data formatting | bytes 4194304
  20.0 2.9 %copy.55 = f32[512,8,128]{0,2,1:T(8,128)} copy(f32[512,8,128]{2,1,0:T(8,128)} %bitcast.68) | data formatting | bytes 4194304 | tf_op jit(solution)/shard_map/reshape | solution.py:11
  22.9 2.2 %reduce_sum.72 = f32[512,8]{1,0:T(8,128)S(1)} reduce(f32[512,8,128]{2,1,0:T(8,128)} %bitcast.69, f32[]{:T(128)} %constant.11.clone.1), dimensions={2}, to_apply=%region_0.0 | reduce | flops 520192 | bytes 2113540 | tf_op jit(solution)/shard_map/reduce_sum | solution.py:12
  25.1 0.1 copy.56
  25.2 0.1 copy.54
  26.0 4.1 %fusion.8 = bf16[512,1024]{1,0:T(8,128)(2,1)} fusion(bf16[512,1024]{1,0:T(8,128)(2,1)} %param.10, bf16[1024,1024]{1,0:T(8,128)(2,1)} %param.13, bf16[512]{0:T(512)(128)(2,1)S(1)} %get-tuple-element.14), kind=kOutput, calls=%fused_computation.25 | convolution fusion | flops 1074790400 | bytes 4195328 | tf_op jit(solution)/shard_map/dot_general | solution.py:46
  30.2 1.5 copy.69
  31.7 0.0 copy-start.3
  31.7 0.0 copy-start.5
  31.7 2.0 %multiply_reduce_fusion = f32[512,8]{0,1:T(8,128)S(1)} fusion(f32[512,8,128]{0,2,1:T(8,128)} %copy.57, f32[512,8]{0,1:T(8,128)S(1)} %broadcast_multiply_fusion.4), kind=kLoop, calls=%fused_computation.17 | loop fusion | flops 1568768 | bytes 2129920 | tf_op jit(solution)/shard_map/reduce_sum | solution.py:13
  33.7 0.2 copy-done.3
  33.9 0.0 copy-start.15
  33.9 0.3 multiply_reduce_fusion.1
  34.2 0.0 copy-done.5
  34.2 1.3 fusion.9
  35.5 0.0 copy-done.1
  35.5 0.0 copy-done.7
  35.5 0.0 copy-done.8
  35.6 0.0 copy-done.14
  35.6 0.0 copy-done.15
  35.6 2.0 %fusion.18 = f32[8,128,128]{2,1,0:T(8,128)} fusion(f32[512,8,128]{0,2,1:T(8,128)S(1)} %copy-done.3, f32[8,128]{1,0:T(8,128)S(1)} %bitcast.83, f32[8,128]{1,0:T(8,128)S(1)} %bitcast.75, f32[512,8]{0,1:T(8,128)S(1)} %get-tuple-element.16, f32[512,8]{0,1:T(8,128)S(1)} %broadcast_multiply_fusion.5, f32[512]{0:T(512)S(1)} %get-tuple-element.13, ...), kind=kOutput, calls=%fused_computation.46 | convolution fusion | flops 140509184 | bytes 4802560 | tf_op jit(solution)/shard_map/nhi,nhj->hij/dot_general | solution.py:43
  37.5 0.0 all-reduce.3.cloned.1.call-update
  37.6 35.9 %psum.22 = f32[]{:T(128)} all-reduce(f32[]{:T(128)S(6)} %convert_element_type.64), channel_id=1, replica_groups=mesh['group'=2,'dx'=16] {'dx'}, use_global_device_ids=true, to_apply=%region_5.0 | all-reduce | flops 1 | bytes 8 | tf_op jit(solution)/shard_map/psum | solution.py:32
  73.5 60.4 %all-reduce.3.cloned.1.call-done = (f32[8,128,128]{2,1,0:T(8,128)}, f32[8,128,128]{2,1,0:T(8,128)}) async-done(((f32[8,128,128]{2,1,0:T(8,128)}, f32[8,128,128]{2,1,0:T(8,128)}), (f32[8,128,128]{2,1,0:T(8,128)}, f32[8,128,128]{2,1,0:T(8,128)})) %all-reduce.3.cloned.1.call-update) | async-done | bytes 1048592 | tf_op jit(solution)/shard_map/psum | solution.py:45
  133.9 4.8 %bitcast_reduce_fusion = (f32[512,8]{0,1:T(8,128)S(1)}, f32[512,8]{0,1:T(8,128)S(1)}, f32[8,128,512]{2,1,0:T(8,128)S(1)}) fusion(f32[8,128]{1,0:T(8,128)S(1)} %bitcast.80, f32[512,8]{0,1:T(8,128)S(1)} %get-tuple-element.15, f32[512,8,128]{0,2,1:T(8,128)} %copy.57, f32[512,8]{0,1:T(8,128)S(1)} %broadcast_multiply_fusion.4, f32[512,8,128]{0,2,1:T(8,128)} %copy.55, ...), kind=kOutput, calls=%fused_computation.2 | convolution fusion | flops 140763136 | bytes 6928388 | tf_op jit(solution)/shard_map/nhi,hij->nhj/dot_general | solution.py:58
  138.7 0.0 copy-done.2
  138.7 0.0 copy-done.4
  138.7 1.7 %bitcast_reduce_fusion.1 = (f32[512,8]{0,1:T(8,128)S(1)}, f32[512,8]{0,1:T(8,128)S(1)}, f32[8,128,512]{2,1,0:T(8,128)S(1)}) fusion(f32[8,128]{1,0:T(8,128)S(1)} %bitcast.77, f32[512,8]{0,1:T(8,128)S(1)} %get-tuple-element.16, f32[512,8,128]{0,2,1:T(8,128)S(1)} %copy-done.4, f32[512,8]{0,1:T(8,128)S(1)} %broadcast_multiply_fusion.5, ...), kind=kOutput, calls=%fused_computation.9 | convolution fusion | flops 140763136 | bytes 6928388 | tf_op jit(solution)/shard_map/nhj,hij->nhi/dot_general | solution.py:57
  140.5 0.8 fusion.6
  141.3 0.0 copy-start.6
  141.3 1.3 fusion.21
  142.6 0.0 copy-start.9
  142.6 1.3 multiply_convert_fusion
  143.9 0.3 copy-done.9
  144.2 1.3 fusion.20
  145.5 0.0 copy-start.10
  145.5 0.8 fusion.2
  146.3 0.8 copy-done.10
  147.1 2.3 %add_convert_fusion = bf16[512,1024]{1,0:T(8,128)(2,1)} fusion(f32[512,1024]{1,0:T(8,128)S(1)} %fusion.20, f32[512,1024]{1,0:T(8,128)S(1)} %fusion.21, bf16[512,1024]{0,1:T(8,128)(2,1)S(1)} %bitcast.73, bf16[1024,1024]{1,0:T(8,128)(2,1)S(1)} %copy-done.10), kind=kOutput, calls=%fused_computation.14 | convolution fusion | flops 1075314688 | bytes 8388608 | tf_op jit(solution)/shard_map/dot_general | solution.py:63
  (20 shorter events, 0.1 us)
Async XLA Ops:
  6.5 10.4 %copy-start = (bf16[1024,1024]{1,0:T(8,128)(2,1)S(1)}, bf16[1024,1024]{1,0:T(8,128)(2,1)}, u32[]{:S(2)}) copy-start(bf16[1024,1024]{1,0:T(8,128)(2,1)} %param.14) | copy-start | bytes 6291460
  6.5 127.3 %all-reduce.3.cloned.1.call-start = ((), (), s32[]{:S(2)}) async-start(), calls=%async_computation | async-start | bytes 2097152 | tf_op jit(solution)/shard_map/psum | solution.py:45
  14.6 2.3 %copy-start.11 = (bf16[512,1024]{1,0:T(8,128)(2,1)S(1)}, bf16[512,1024]{1,0:T(8,128)(2,1)}, u32[]{:S(2)}) copy-start(bf16[512,1024]{1,0:T(8,128)(2,1)} %param.10) | copy-start | bytes 3145732
  31.7 2.2 %copy-start.3 = (f32[512,8,128]{0,2,1:T(8,128)S(1)}, f32[512,8,128]{0,2,1:T(8,128)}, u32[]{:S(2)}) copy-start(f32[512,8,128]{0,2,1:T(8,128)} %copy.55) | copy-start | bytes 6291460
  31.7 2.6 %copy-start.5 = (bf16[512,1024]{1,0:T(8,128)(2,1)S(1)}, bf16[512,1024]{1,0:T(8,128)(2,1)}, u32[]{:S(2)}) copy-start(bf16[512,1024]{1,0:T(8,128)(2,1)} %param.11) | copy-start | bytes 3145732
  33.9 1.7 %copy-start.1 = (f32[512,8,128]{0,2,1:T(8,128)S(1)}, f32[512,8,128]{0,2,1:T(8,128)}, u32[]{:S(2)}) copy-start(f32[512,8,128]{0,2,1:T(8,128)} %copy.57) | copy-start | bytes 6291460
  33.9 1.7 %copy-start.7 = (f32[1024]{0:T(1024)S(1)}, f32[1024]{0:T(1024)}, u32[]{:S(2)}) copy-start(f32[1024]{0:T(1024)} %param.16) | copy-start | bytes 12292
  33.9 1.7 %copy-start.8 = (f32[1024]{0:T(1024)S(1)}, f32[1024]{0:T(1024)}, u32[]{:S(2)}) copy-start(f32[1024]{0:T(1024)} %param.18) | copy-start | bytes 12292
  33.9 1.7 %copy-start.14 = (f32[1024]{0:T(1024)S(1)}, f32[1024]{0:T(1024)}, u32[]{:S(2)}) copy-start(f32[1024]{0:T(1024)} %param.17) | copy-start | bytes 12292
  33.9 1.7 %copy-start.15 = (f32[1024]{0:T(1024)S(1)}, f32[1024]{0:T(1024)}, u32[]{:S(2)}) copy-start(f32[1024]{0:T(1024)} %param.19) | copy-start | bytes 12292
  133.9 4.8 %copy-start.2 = (f32[512,8,128]{0,2,1:T(8,128)S(1)}, f32[512,8,128]{0,2,1:T(8,128)}, u32[]{:S(2)}) copy-start(f32[512,8,128]{0,2,1:T(8,128)} %copy.57) | copy-start | bytes 6291460
  133.9 4.8 %copy-start.4 = (f32[512,8,128]{0,2,1:T(8,128)S(1)}, f32[512,8,128]{0,2,1:T(8,128)}, u32[]{:S(2)}) copy-start(f32[512,8,128]{0,2,1:T(8,128)} %copy.55) | copy-start | bytes 6291460
  133.9 4.8 %copy-start.13 = (f32[8,128,128]{2,1,0:T(8,128)S(1)}, f32[8,128,128]{2,1,0:T(8,128)}, u32[]{:S(2)}) copy-start(f32[8,128,128]{2,1,0:T(8,128)} %get-tuple-element.10) | copy-start | bytes 1572868
  141.3 1.4 copy-start.6
  141.3 1.4 copy-start.12
  142.6 1.6 %copy-start.9 = (bf16[1024,1024]{1,0:T(8,128)(2,1)S(1)}, bf16[1024,1024]{1,0:T(8,128)(2,1)}, u32[]{:S(2)}) copy-start(bf16[1024,1024]{1,0:T(8,128)(2,1)} %param.13) | copy-start | bytes 6291460
  145.5 1.6 %copy-start.10 = (bf16[1024,1024]{1,0:T(8,128)(2,1)S(1)}, bf16[1024,1024]{1,0:T(8,128)(2,1)}, u32[]{:S(2)}) copy-start(bf16[1024,1024]{1,0:T(8,128)(2,1)} %param.15) | copy-start | bytes 6291460
Sparse Core Ops, SparseCore 0:
  37.7 96.1 all-reduce.2
where the time goes:
time: 157 us; the launch traced here: 156 us
  waiting for transfers between devices  60.4 us (38%)
  blocking collectives  35.9 us (23%)
  matrix products  24.6 us (16%)
  between operations  14.3 us (9%)
  local copies, waits for them, and re-layouts  12.5 us (8%)
  other arithmetic  8.47 us (5%)
    psum x1, waiting for transfers between devices, body(): kv_sum = lax.psum(kv_local, 'dx')  60.4 us
    psum x1, blocking collectives, body(): total = lax.psum(own_count, 'dx')  35.9 us
    reshape x2, local copies, waits for them, and re-layouts, head_norm(): grouped = raw.reshape(raw.shape[0], heads, -1)  5.92 us
    unnamed x34, local copies, waits for them, and re-layouts  4.87 us
    dot_general x1, matrix products, body(): jnp.einsum('nhi,hij->nhj', keys, dgram, preferred_element_type=jnp.float32)  4.81 us
    reduce_sum x2, other arithmetic, head_norm(): center = grouped - jnp.mean(grouped, axis=2, keepdims=True)  4.51 us
    dot_general x1, matrix products, body(): jnp.dot(points, w_query, preferred_element_type=jnp.float32)  4.15 us
    dot_general x1, matrix products, body(): jnp.dot(points, w_value, preferred_element_type=jnp.float32)  3.3 us
  transfers between devices with their start and end apart: 1, of which 1 were waited for; matrix products, arithmetic and copies ran while one was open for 0% of the time, Pallas kernels for 0%

commit v1 on v0

--- a/solution.py
+++ b/solution.py
@@ -42,7 +42,7 @@
     ).astype(jnp.bfloat16)
     kv_local = jnp.einsum("nhi,nhj->hij", keys, values, preferred_element_type=jnp.float32)
     cot = cotangent.reshape(rows, heads, -1)
-    kv_sum = lax.psum(kv_local, "dx")
+    kv_sum = jnp.sum(lax.all_gather(kv_local, "dx"), axis=0)
     query = jnp.dot(points, w_query, preferred_element_type=jnp.float32).astype(jnp.bfloat16)
     masked_query = (query * live.astype(jnp.bfloat16)).reshape(rows, heads, -1)
     qdy_local = jnp.einsum("nhi,nhj->hij", masked_query, cot, preferred_element_type=jnp.float32)

time: 157 us -> 205 us (1.31)
  waiting for transfers between devices: 60.4 us -> 99.6 us
  other arithmetic: 8.47 us -> 14.3 us
  matrix products: 24.6 us -> 27.7 us
    all_gather x0 -> x1, waiting for transfers between devices: none -> 66 us  [body(): kv_sum = jnp.sum(lax.all_gather(kv_local, 'dx'), axis=0)]
    psum x1, waiting for transfers between devices: 60.4 us -> 33.6 us  [body(): qdy_sum = lax.psum(qdy_local, 'dx')]
    reduce_sum x0 -> x1, other arithmetic: none -> 4.85 us  [body(): kv_sum = jnp.sum(lax.all_gather(kv_local, 'dx'), axis=0)]
  transfers between devices with their start and end apart: 1 -> 2, of which waited for: 1 -> 2; matrix products, arithmetic and copies ran while one was open for 0% -> 17% of each run, Pallas kernels for 0% -> 0%
where the time goes in v1:
time: 205 us
  waiting for transfers between devices  99.6 us (49%)
  blocking collectives  35.8 us (17%)
  matrix products  27.7 us (14%)
  between operations  14.5 us (7%)
  other arithmetic  14.3 us (7%)
  local copies, waits for them, and re-layouts  12.9 us (6%)
    all_gather x1, waiting for transfers between devices, body(): kv_sum = jnp.sum(lax.all_gather(kv_local, 'dx'), axis=0)  66 us
    psum x1, blocking collectives, body(): total = lax.psum(own_count, 'dx')  35.8 us
    psum x1, waiting for transfers between devices, body(): qdy_sum = lax.psum(qdy_local, 'dx')  33.6 us
    reshape x2, local copies, waits for them, and re-layouts, head_norm(): grouped = raw.reshape(raw.shape[0], heads, -1)  5.86 us
    unnamed x34, local copies, waits for them, and re-layouts  5.33 us
    reduce_sum x1, other arithmetic, body(): kv_sum = jnp.sum(lax.all_gather(kv_local, 'dx'), axis=0)  4.85 us
    dot_general x1, matrix products, body(): jnp.einsum('nhi,hij->nhj', keys, dgram, preferred_element_type=jnp.float32)  4.64 us
    reduce_sum x2, other arithmetic, head_norm(): center = grouped - jnp.mean(grouped, axis=2, keepdims=True)  4.53 us
  transfers between devices with their start and end apart: 2, of which 2 were waited for; matrix products, arithmetic and copies ran while one was open for 17% of the time, Pallas kernels for 0%

profile of v1, /device:TPU:0, one launch (start us, length us, event | category | flops | bytes accessed | tf_op | source)
XLA Modules:
  0.0 204.9 jit_solution(13449697773431012890)
XLA Ops:
  6.5 0.0 all-reduce.2.cloned.1.call-start
  7.4 4.1 %fusion.8 = bf16[512,1024]{1,0:T(8,128)(2,1)} fusion(bf16[512,1024]{1,0:T(8,128)(2,1)} %param.10, bf16[1024,1024]{1,0:T(8,128)(2,1)} %param.13, bf16[512]{0:T(512)(128)(2,1)S(1)} %fusion.16), kind=kOutput, calls=%fused_computation.25 | convolution fusion | flops 1074790400 | bytes 4195328 | tf_op jit(solution)/shard_map/dot_general | solution.py:46
  11.5 1.5 copy.71
  13.0 2.5 %fusion.9 = f32[8,128,128]{2,1,0:T(8,128)} fusion(bf16[512,8,128]{0,2,1:T(8,128)(2,1)S(1)} %bitcast.75, bf16[512,1024]{1,0:T(8,128)(2,1)} %param.11), kind=kOutput, calls=%fused_computation.26 | convolution fusion | flops 134217728 | bytes 2621440 | tf_op jit(solution)/shard_map/nhi,nhj->hij/dot_general | solution.py:48
  15.5 0.0 all-reduce.2.cloned.1.call-update
  15.5 0.0 all-gather.3.cloned.1.call-start
  15.6 3.2 %convolution_bitcast_fusion = f32[64,8,8,128]{3,1,2,0:T(8,128)S(1)} fusion(bf16[512,1024]{1,0:T(8,128)(2,1)} %param.10, bf16[1024,1024]{1,0:T(8,128)(2,1)} %param.15), kind=kOutput, calls=%fused_computation.22 | convolution fusion | flops 1073741824 | bytes 5242880 | tf_op jit(solution)/shard_map/dot_general | solution.py:35
  18.7 1.8 copy.74
  20.5 3.0 %copy.59 = f32[512,8,128]{0,2,1:T(8,128)} copy(f32[512,8,128]{2,1,0:T(8,128)} %bitcast.70) | data formatting | bytes 4194304 | tf_op jit(solution)/shard_map/reshape | solution.py:11
  23.5 2.3 %reduce_sum.83 = f32[512,8]{1,0:T(8,128)S(1)} reduce(f32[512,8,128]{2,1,0:T(8,128)} %bitcast.71, f32[]{:T(128)} %constant.11.clone.1), dimensions={2}, to_apply=%region_2.0 | reduce | flops 520192 | bytes 2113540 | tf_op jit(solution)/shard_map/reduce_sum | solution.py:12
  25.8 0.0 copy-done
  25.8 0.0 copy-done.11
  25.8 1.3 convolution_bitcast_fusion.1
  27.1 1.8 copy.73
  28.9 2.9 %copy.57 = f32[512,8,128]{0,2,1:T(8,128)} copy(f32[512,8,128]{2,1,0:T(8,128)} %bitcast.72) | data formatting | bytes 4194304 | tf_op jit(solution)/shard_map/reshape | solution.py:11
  31.8 2.2 %reduce_sum.81 = f32[512,8]{1,0:T(8,128)S(1)} reduce(f32[512,8,128]{2,1,0:T(8,128)} %bitcast.73, f32[]{:T(128)} %constant.11.clone.1), dimensions={2}, to_apply=%region_0.0 | reduce | flops 520192 | bytes 2113540 | tf_op jit(solution)/shard_map/reduce_sum | solution.py:12
  34.0 0.1 copy.58
  34.1 0.1 copy.56
  34.3 0.0 copy-start.7
  34.3 0.0 copy-start.8
  34.3 0.0 copy-start.13
  34.3 0.0 copy-start.14
  34.3 2.1 %multiply_reduce_fusion = f32[512,8]{0,1:T(8,128)S(1)} fusion(f32[512,8,128]{0,2,1:T(8,128)} %copy.59, f32[512,8]{0,1:T(8,128)S(1)} %broadcast_multiply_fusion.4), kind=kLoop, calls=%fused_computation.17 | loop fusion | flops 1568768 | bytes 2129920 | tf_op jit(solution)/shard_map/reduce_sum | solution.py:13
  36.4 0.1 copy-done.1
  36.5 0.3 multiply_reduce_fusion.1
  36.8 0.3 copy-done.3
  37.1 0.0 copy-done.7
  37.1 0.0 copy-done.13
  37.1 2.0 fusion.18
  39.1 0.0 all-gather.3.cloned.1.call-update
  39.2 35.8 %psum.14 = f32[]{:T(128)} all-reduce(f32[]{:T(128)S(6)} %convert_element_type.64), channel_id=1, replica_groups=mesh['group'=2,'dx'=16] {'dx'}, use_global_device_ids=true, to_apply=%region_5.0 | all-reduce | flops 1 | bytes 8 | tf_op jit(solution)/shard_map/psum | solution.py:32
  75.0 33.6 %all-reduce.2.cloned.1.call-done = f32[8,128,128]{2,1,0:T(8,128)} async-done(((f32[8,128,128]{2,1,0:T(8,128)}), f32[8,128,128]{2,1,0:T(8,128)}) %all-reduce.2.cloned.1.call-update) | async-done | bytes 524304 | tf_op jit(solution)/shard_map/psum | solution.py:49
  108.5 4.6 %bitcast_reduce_fusion = (f32[512,8]{0,1:T(8,128)S(1)}, f32[512,8]{0,1:T(8,128)S(1)}, f32[8,128,512]{2,1,0:T(8,128)S(1)}) fusion(f32[8,128]{1,0:T(8,128)S(1)} %bitcast.79, f32[512,8]{0,1:T(8,128)S(1)} %get-tuple-element.11, f32[512,8,128]{0,2,1:T(8,128)} %copy.59, f32[512,8]{0,1:T(8,128)S(1)} %broadcast_multiply_fusion.4, f32[512,8,128]{0,2,1:T(8,128)} %copy.57, ...), kind=kOutput, calls=%fused_computation.2 | convolution fusion | flops 140763136 | bytes 6928388 | tf_op jit(solution)/shard_map/nhi,hij->nhj/dot_general | solution.py:58
  113.2 0.0 copy-done.2
  113.2 0.0 copy-done.4
  113.2 1.6 bitcast_reduce_fusion.1
  114.8 1.8 fusion.2
  116.6 0.8 fusion.6
  117.4 2.7 %fusion.21 = f32[512,1024]{1,0:T(8,128)} fusion(bf16[512,1024]{0,1:T(8,128)(2,1)S(1)} %bitcast.77, bf16[1024,1024]{1,0:T(8,128)(2,1)S(1)} %copy-done), kind=kOutput, calls=%fused_computation.49 | convolution fusion | flops 1073741824 | bytes 5242880 | tf_op jit(solution)/shard_map/dot_general | solution.py:62
  120.1 66.0 %all-gather.3.cloned.1.call-done = f32[128,128,128]{2,1,0:T(8,128)} async-done(((f32[8,128,128]{2,1,0:T(8,128)}), f32[128,128,128]{2,1,0:T(8,128)}) %all-gather.3.cloned.1.call-update) | async-done | bytes 8388624 | tf_op jit(solution)/shard_map/all_gather | solution.py:45
  186.1 4.8 %reduce_sum.85 = f32[8,128,128]{2,1,0:T(8,128)} reduce(f32[16,8,128,128]{3,2,1,0:T(8,128)} %bitcast.74, f32[]{:T(128)} %constant.11.clone.1), dimensions={0}, to_apply=%region_4.0 | reduce | flops 1966080 | bytes 8912900 | tf_op jit(solution)/shard_map/reduce_sum | solution.py:45
  191.0 2.2 %multiply_convert_fusion = bf16[8,128,512]{2,1,0:T(8,128)(2,1)S(1)} fusion(f32[512]{0:T(512)S(1)} %fusion.15, f32[8,128,128]{2,1,0:T(8,128)} %reduce_sum.85, f32[]{:T(128)} %psum.14, bf16[512,1024]{1,0:T(8,128)(2,1)S(1)} %copy-done.5), kind=kOutput, calls=%fused_computation.15 | convolution fusion | flops 135528448 | bytes 2623492 | tf_op jit(solution)/shard_map/nhj,hij->nhi/dot_general | solution.py:53
  193.2 0.0 copy-start.6
  193.2 0.0 copy-start.10
  193.2 1.3 fusion.20
  194.5 0.6 copy-done.10
  195.1 0.6 copy-done.15
  195.8 2.3 %add_convert_fusion = bf16[512,1024]{1,0:T(8,128)(2,1)} fusion(f32[512,1024]{1,0:T(8,128)S(1)} %fusion.20, f32[512,1024]{1,0:T(8,128)S(1)} %copy-done.15, bf16[512,1024]{0,1:T(8,128)(2,1)S(1)} %bitcast.76, bf16[1024,1024]{1,0:T(8,128)(2,1)S(1)} %copy-done.10), kind=kOutput, calls=%fused_computation.14 | convolution fusion | flops 1075314688 | bytes 8388608 | tf_op jit(solution)/shard_map/dot_general | solution.py:63
  (25 shorter events, 0.1 us)
Async XLA Ops:
  6.5 19.3 %copy-start = (bf16[1024,1024]{1,0:T(8,128)(2,1)S(1)}, bf16[1024,1024]{1,0:T(8,128)(2,1)}, u32[]{:S(2)}) copy-start(bf16[1024,1024]{1,0:T(8,128)(2,1)} %param.14) | copy-start | bytes 6291460
  6.5 102.0 %all-reduce.2.cloned.1.call-start = ((), (), s32[]{:S(2)}) async-start(), calls=%async_computation | async-start | bytes 1048576 | tf_op jit(solution)/shard_map/psum | solution.py:49
  15.5 170.6 %all-gather.3.cloned.1.call-start = ((), (), s32[]{:S(2)}) async-start(), calls=%async_computation.1 | async-start | bytes 8912896 | tf_op jit(solution)/shard_map/all_gather | solution.py:45
  23.5 2.3 %copy-start.11 = (bf16[512,1024]{1,0:T(8,128)(2,1)S(1)}, bf16[512,1024]{1,0:T(8,128)(2,1)}, u32[]{:S(2)}) copy-start(bf16[512,1024]{1,0:T(8,128)(2,1)} %param.10) | copy-start | bytes 3145732
  34.2 2.3 %copy-start.1 = (f32[512,8,128]{0,2,1:T(8,128)S(1)}, f32[512,8,128]{0,2,1:T(8,128)}, u32[]{:S(2)}) copy-start(f32[512,8,128]{0,2,1:T(8,128)} %copy.57) | copy-start | bytes 6291460
  34.3 2.9 %copy-start.3 = (f32[512,8,128]{0,2,1:T(8,128)S(1)}, f32[512,8,128]{0,2,1:T(8,128)}, u32[]{:S(2)}) copy-start(f32[512,8,128]{0,2,1:T(8,128)} %copy.59) | copy-start | bytes 6291460
  34.3 2.9 %copy-start.7 = (f32[1024]{0:T(1024)S(1)}, f32[1024]{0:T(1024)}, u32[]{:S(2)}) copy-start(f32[1024]{0:T(1024)} %param.18) | copy-start | bytes 12292
  34.3 2.8 %copy-start.8 = (f32[1024]{0:T(1024)S(1)}, f32[1024]{0:T(1024)}, u32[]{:S(2)}) copy-start(f32[1024]{0:T(1024)} %param.16) | copy-start | bytes 12292
  34.3 2.8 %copy-start.13 = (f32[1024]{0:T(1024)S(1)}, f32[1024]{0:T(1024)}, u32[]{:S(2)}) copy-start(f32[1024]{0:T(1024)} %param.17) | copy-start | bytes 12292
  34.3 2.8 %copy-start.14 = (f32[1024]{0:T(1024)S(1)}, f32[1024]{0:T(1024)}, u32[]{:S(2)}) copy-start(f32[1024]{0:T(1024)} %param.19) | copy-start | bytes 12292
  108.5 4.7 %copy-start.2 = (f32[512,8,128]{0,2,1:T(8,128)S(1)}, f32[512,8,128]{0,2,1:T(8,128)}, u32[]{:S(2)}) copy-start(f32[512,8,128]{0,2,1:T(8,128)} %copy.57) | copy-start | bytes 6291460
  108.5 4.7 %copy-start.4 = (f32[512,8,128]{0,2,1:T(8,128)S(1)}, f32[512,8,128]{0,2,1:T(8,128)}, u32[]{:S(2)}) copy-start(f32[512,8,128]{0,2,1:T(8,128)} %copy.59) | copy-start | bytes 6291460
  108.5 4.7 %copy-start.12 = (f32[8,128,128]{2,1,0:T(8,128)S(1)}, f32[8,128,128]{2,1,0:T(8,128)}, u32[]{:S(2)}) copy-start(f32[8,128,128]{2,1,0:T(8,128)} %all-reduce.2.cloned.1.call-done) | copy-start | bytes 1572868
  186.1 4.9 %copy-start.5 = (bf16[512,1024]{1,0:T(8,128)(2,1)S(1)}, bf16[512,1024]{1,0:T(8,128)(2,1)}, u32[]{:S(2)}) copy-start(bf16[512,1024]{1,0:T(8,128)(2,1)} %param.11) | copy-start | bytes 3145732
  191.0 2.2 %copy-start.9 = (bf16[1024,1024]{1,0:T(8,128)(2,1)S(1)}, bf16[1024,1024]{1,0:T(8,128)(2,1)}, u32[]{:S(2)}) copy-start(bf16[1024,1024]{1,0:T(8,128)(2,1)} %param.13) | copy-start | bytes 6291460
  193.2 1.3 copy-start.6
  193.2 1.9 copy-start.10
  193.2 2.5 %copy-start.15 = (f32[512,1024]{1,0:T(8,128)S(1)}, f32[512,1024]{1,0:T(8,128)}, u32[]{:S(2)}) copy-start(f32[512,1024]{1,0:T(8,128)} %fusion.21) | copy-start | bytes 6291460
Sparse Core Ops, SparseCore 0:
  15.6 92.8 all-reduce.1
  110.7 75.3 all-gather.2
